TPU v7x, 256 devices: a whole 4x4x8 slice. The times are simulated.
256 devices in a mesh: slot: 16 (over z, core), hid: 16 (over y, x).
Axes of the slice: x: 4, y: 4, z: 8, core: 2. Of those that a mesh axis runs over, the one named last changes fastest.
Arguments:
- cotangent: bfloat16 [32768, 2048], P('slot', 'hid'), may hold values from -6 to 6
- hidden: bfloat16 [32768, 8192], P('slot', 'hid'), may hold values from -6 to 6
- weights: bfloat16 [16, 8192, 2048], P('slot', 'hid'), may hold values from -0.125 to 0.125
- slot_experts: int32 [16, 1], replicated, may hold values from 0 to 3
- next_experts: int32 [16, 1], replicated, may hold values from 0 to 3
- row_counts: int32 [16], replicated, may hold values from 1 to 2048, 20480 in all
- master: float32 [4, 8192, 2048], P(None, 'hid', 'slot'), may hold values from -3 to 3
- momentum: float32 [4, 8192, 2048], P(None, 'hid', 'slot'), may hold values from -96 to 96
Outputs:
- input_grad: bfloat16 [32768, 8192], P('slot', 'hid')
- new_momentum: float32 [4, 8192, 2048], P(None, 'hid', 'slot')
- new_master: float32 [4, 8192, 2048], P(None, 'hid', 'slot')
- placed: bfloat16 [16, 8192, 2048], P('slot', 'hid')
Inputs may be any that keep to these rules, and one draw needn't show every extreme that they name: `slot_experts`: every expert 0 to 3 is held by at least one slot. `next_experts`: every expert 0 to 3 is held by at least one slot. `row_counts`: the counts sum to 20480.
All inputs are finite; a program needn't handle non-finite values.
Results may differ from a plain program's by a relative error of at most 0.015.
Values may be sent and summed in bfloat16 or wider, within the bound.
No kernel may reach another device: no remote copies, remote signals or barrier semaphores. Data moves between devices by JAX's collectives and lax.ppermute only.
A program may use at most 128 MiB of HBM per device.

v0:
```python
import jax
import jax.numpy as jnp
from jax import lax
from jax.sharding import PartitionSpec as P

momentum_decay = 0.9
learn_rate = 0.01


def local(cotangent, hidden, weights, slot_experts, next_experts, row_counts, master, momentum):
    row_span = hidden.shape[0]
    own_slot = lax.axis_index("slot")
    live_count = lax.dynamic_index_in_dim(row_counts, own_slot, 0, keepdims=False)
    live_mask = (jnp.arange(row_span, dtype=jnp.int32) < live_count)[:, None].astype(
        cotangent.dtype
    )
    masked = cotangent * live_mask
    weight_rows = weights[0]
    shard_piece = lax.all_gather(masked, "hid", axis=1, tiled=True)
    hid_grad = lax.dot_general(
        shard_piece, weight_rows, (((1,), (1,)), ((), ())), preferred_element_type=jnp.float32
    )
    w_part = lax.dot_general(
        hidden, shard_piece, (((0,), (0,)), ((), ())), preferred_element_type=jnp.float32
    )
    w_grad = w_part
    hid_grad, w_grad = (hid_grad, w_grad)
    input_grad = hid_grad.astype(jnp.bfloat16)
    expert_count = master.shape[0]
    owners = (
        slot_experts[:, 0][None, :] == jnp.arange(expert_count, dtype=jnp.int32)[:, None]
    ).astype(jnp.float32)
    own_weight = lax.dynamic_index_in_dim(owners, own_slot, 1, keepdims=False)
    stacked = own_weight[:, None, None] * w_grad[None]
    expert_grad = lax.psum_scatter(
        stacked.astype(jnp.bfloat16), "slot", scatter_dimension=2, tiled=True
    ).astype(jnp.float32)
    new_momentum = momentum_decay * momentum + expert_grad
    new_master = master - learn_rate * new_momentum
    rounded = new_master.astype(jnp.bfloat16)
    gathered = lax.all_gather(rounded, "slot", axis=2, tiled=True)
    target = lax.dynamic_index_in_dim(next_experts[:, 0], own_slot, 0, keepdims=False)
    placed = lax.dynamic_index_in_dim(gathered, target, 0, keepdims=True)
    return (input_grad, new_momentum, new_master, placed)


def solution(mesh):
    return jax.shard_map(
        local,
        mesh=mesh,
        in_specs=(
            P("slot", "hid"),
            P("slot", "hid"),
            P("slot", "hid", None),
            P(),
            P(),
            P(),
            P(None, "hid", "slot"),
            P(None, "hid", "slot"),
        ),
        out_specs=(
            P("slot", "hid"),
            P(None, "hid", "slot"),
            P(None, "hid", "slot"),
            P("slot", "hid", None),
        ),
        check_vma=False,
    )
```

profile of v0, /device:TPU:1, one launch (start us, length us, event | category | flops | bytes accessed | tf_op | source)
XLA Modules:
  0.0 297.3 jit_solution(14528464055429409936)
XLA Ops:
  7.2 0.0 copy-start
  7.2 0.0 all-gather.3.cloned.1.call-start
  7.2 1.4 dynamic_slice.15
  8.6 0.6 fusion.1
  9.3 2.2 broadcast_multiply_fusion
  11.4 0.0 all-gather.3.cloned.1.call-update
  11.5 0.0 reduce-scatter.4.cloned.1.call-start
  11.5 1.2 dynamic-slice.1
  12.8 0.6 fusion.2
  13.4 84.5 %all-gather.3.cloned.1.call-done = bf16[2048,2048]{1,0:T(8,128)(2,1)} async-done(((bf16[2048,128]{1,0:T(8,128)(2,1)}), bf16[2048,2048]{1,0:T(8,128)(2,1)}) %all-gather.3.cloned.1.call-update) | async-done | bytes 8388624 | tf_op jit(solution)/shard_map/all_gather | solution.py:19
  97.9 0.0 copy-done
  97.9 9.8 %convolution_bitcast_fusion = f32[512,2048]{0,1:T(8,128)} fusion(bf16[2048,2048]{1,0:T(8,128)(2,1)} %all-gather.3.cloned.1.call-done, bf16[2048,512]{1,0:T(8,128)(2,1)S(1)} %copy-done), kind=kOutput, calls=%fused_computation.1 | convolution fusion | flops 4294967296 | bytes 14680064 | tf_op jit(solution)/shard_map/dot_general | solution.py:23
  107.7 5.5 %copy.13 = f32[512,2048]{1,0:T(8,128)} copy(f32[512,2048]{0,1:T(8,128)} %convolution_bitcast_fusion) | data formatting | bytes 8388608 | tf_op jit(solution)/shard_map/dot_general | solution.py:23
  113.1 8.0 %multiply_convert_fusion = bf16[4,512,2048]{2,1,0:T(8,128)(2,1)} fusion(f32[512,2048]{1,0:T(8,128)} %copy.13, f32[4]{0:T(128)S(1)} %fusion.2), kind=kLoop, calls=%fused_computation | loop fusion | flops 8388608 | bytes 12582928 | tf_op jit(solution)/shard_map/convert_element_type | solution.py:36
  121.1 14.6 %copy.14 = bf16[4,512,2048]{1,0,2:T(4,128)(2,1)} copy(bf16[4,512,2048]{2,1,0:T(8,128)(2,1)} %multiply_convert_fusion) | data formatting | bytes 16777216
  135.7 10.2 %copy.16 = bf16[256,8,4,512]{3,1,2,0:T(8,128)(2,1)} copy(bf16[256,8,4,512]{3,2,1,0:T(4,128)(2,1)} %bitcast.18) | data formatting | bytes 16777216
  146.0 0.0 reduce-scatter.4.cloned.1.call-update
  146.0 0.0 copy-start.1
  146.0 0.2 all-gather.5.cloned.1.call-start
  146.2 68.0 %reduce-scatter.4.cloned.1.call-done = bf16[128,2048]{1,0:T(8,128)(2,1)} async-done(((bf16[2048,2048]{1,0:T(8,128)(2,1)}), bf16[128,2048]{1,0:T(8,128)(2,1)}) %reduce-scatter.4.cloned.1.call-update) | async-done | bytes 524304
  214.3 1.4 reshape.21
  215.7 0.4 copy.15
  216.1 3.2 %fusion.3 = (bf16[4,512,128]{2,1,0:T(8,128)(2,1)}, f32[4,512,128]{2,1,0:T(8,128)}, f32[4,512,128]{2,1,0:T(8,128)}) fusion(f32[4,512,128]{2,1,0:T(8,128)} %param.14, bf16[4,512,128]{2,1,0:T(8,128)(2,1)S(1)} %copy.15, f32[4,512,128]{2,1,0:T(8,128)} %param.15), kind=kLoop, calls=%fused_computation.13 | loop fusion | flops 1572864 | bytes 5242880 | tf_op jit(solution)/shard_map/convert_element_type | solution.py:40
  219.4 0.0 all-gather.5.cloned.1.call-update
  219.4 0.0 copy-done.1
  219.4 0.6 constant_dynamic-slice_fusion
  221.9 9.9 %convolution_convert_fusion = bf16[2048,512]{1,0:T(8,128)(2,1)} fusion(bf16[2048,2048]{1,0:T(8,128)(2,1)} %all-gather.3.cloned.1.call-done, bf16[1,512,2048]{2,1,0:T(8,128)(2,1)} %param.10), kind=kOutput, calls=%fused_computation.2 | convolution fusion | flops 4296015872 | bytes 12582912 | tf_op jit(solution)/shard_map/dot_general | solution.py:20
  231.8 55.9 %all-gather.5.cloned.1.call-done = bf16[4,512,2048]{2,1,0:T(8,128)(2,1)} async-done(((bf16[4,512,128]{2,1,0:T(8,128)(2,1)}), bf16[4,512,2048]{2,1,0:T(8,128)(2,1)}) %all-gather.5.cloned.1.call-update) | async-done | bytes 8388624 | tf_op jit(solution)/shard_map/all_gather | solution.py:41
  287.6 3.2 %constant_dynamic-slice_fusion.1 = bf16[1,512,2048]{2,1,0:T(8,128)(2,1)} fusion(bf16[4,512,2048]{2,1,0:T(8,128)(2,1)} %all-gather.5.cloned.1.call-done, s32[]{:T(128)S(6)} %select_n.12), kind=kLoop, calls=%fused_computation.12 | loop fusion | bytes 4194308 | tf_op jit(solution)/shard_map/jit(dynamic_index_in_dim)/dynamic_slice | solution.py:43
Async XLA Ops:
  7.2 90.8 %copy-start = (bf16[2048,512]{1,0:T(8,128)(2,1)S(1)}, bf16[2048,512]{1,0:T(8,128)(2,1)}, u32[]{:S(2)}) copy-start(bf16[2048,512]{1,0:T(8,128)(2,1)} %param.9) | copy-start | bytes 6291460
  7.2 90.7 %all-gather.3.cloned.1.call-start = ((), (), s32[]{:S(2)}) async-start(), calls=%async_computation.1 | async-start | bytes 8912896 | tf_op jit(solution)/shard_map/all_gather | solution.py:19
  11.5 202.8 %reduce-scatter.4.cloned.1.call-start = ((), (), s32[]{:S(2)}) async-start(), calls=%async_computation.3 | async-start | bytes 8912896
  146.0 73.4 %copy-start.1 = (s32[16,1]{0,1:T(1,128)S(1)}, s32[16,1]{0,1:T(1,128)}, u32[]{:S(2)}) copy-start(s32[16,1]{0,1:T(1,128)} %param.12) | copy-start | bytes 196
  146.0 141.6 %all-gather.5.cloned.1.call-start = ((), (), s32[]{:S(2)}) async-start(), calls=%async_computation.2 | async-start | bytes 8912896 | tf_op jit(solution)/shard_map/all_gather | solution.py:41
Sparse Core Ops, SparseCore 0:
  11.6 86.2 all-gather.2
  146.1 68.1 reduce-scatter.3
  219.5 68.0 all-gather.4
where the time goes:
time: 298 us; the launch traced here: 297 us
  waiting for transfers between devices  208 us (70%)
  local copies, waits for them, and re-layouts  38.5 us (13%)
  matrix products  19.6 us (7%)
  between operations  15.7 us (5%)
  other arithmetic  14.7 us (5%)
    all_gather x1, waiting for transfers between devices, local(): shard_piece = lax.all_gather(masked, 'hid', axis=1, tiled=True)  84.5 us
    unnamed x4, waiting for transfers between devices  68.1 us
    all_gather x1, waiting for transfers between devices, local(): gathered = lax.all_gather(rounded, 'slot', axis=2, tiled=True)  55.9 us
    unnamed x8, local copies, waits for them, and re-layouts  26.7 us
    dot_general x1, matrix products, local(): lax.dot_general(shard_piece, weight_rows, (((1,), (1,)), ((), ())), prefe...  9.86 us
    dot_general x1, matrix products, local(): lax.dot_general(hidden, shard_piece, (((0,), (0,)), ((), ())), preferred_...  9.75 us
    convert_element_type x1, other arithmetic, local(): stacked.astype(jnp.bfloat16)  8 us
  transfers between devices with their start and end apart: 3, of which 3 were waited for; matrix products, arithmetic and copies ran while one was open for 4% of the time, Pallas kernels for 0%

commit v1 on v0

--- a/solution.py
+++ b/solution.py
@@ -16,7 +16,9 @@
     )
     masked = cotangent * live_mask
     weight_rows = weights[0]
-    shard_piece = lax.all_gather(masked, "hid", axis=1, tiled=True)
+    shard_piece = jnp.concatenate(
+        lax.all_to_all(jnp.stack([masked] * lax.axis_size("hid")), "hid", 0, 0), axis=1
+    )
     hid_grad = lax.dot_general(
         shard_piece, weight_rows, (((1,), (1,)), ((), ())), preferred_element_type=jnp.float32
     )

time: 298 us -> 347 us (1.16)
  waiting for transfers between devices: 208 us -> 248 us
  starting transfers between devices: 0.3 us -> 8.03 us
  local copies, waits for them, and re-layouts: 38.5 us -> 42.4 us
    all_to_all x0 -> x1, waiting for transfers between devices: none -> 122 us  [local(): lax.all_to_all(jnp.stack([masked] * lax.axis_size('hid')), 'hid', 0, 0)]
    all_gather x1 -> x0, waiting for transfers between devices: 84.5 us -> none  [local(): shard_piece = lax.all_gather(masked, 'hid', axis=1, tiled=True)]
    all_to_all x0 -> x1, starting transfers between devices: none -> 7.77 us  [local(): lax.all_to_all(jnp.stack([masked] * lax.axis_size('hid')), 'hid', 0, 0)]
    another operation x0 -> x1, local copies, waits for them, and re-layouts: none -> 4.33 us  [local(): jnp.stack([masked] * lax.axis_size('hid'))]
    unnamed x4 -> x3, waiting for transfers between devices: 68.1 us -> 70.4 us
    unnamed x8 -> x16, local copies, waits for them, and re-layouts: 26.7 us -> 26.7 us
  transfers between devices with their start and end apart: 3 -> 3, of which waited for: 3 -> 3; matrix products, arithmetic and copies ran while one was open for 4% -> 3% of each run, Pallas kernels for 0% -> 0%
where the time goes in v1:
time: 347 us; the launch traced here: 346 us
  waiting for transfers between devices  248 us (71%)
  local copies, waits for them, and re-layouts  42.4 us (12%)
  matrix products  19.5 us (6%)
  between operations  16.1 us (5%)
  other arithmetic  12.4 us (4%)
  starting transfers between devices  8.03 us (2%)
    all_to_all x1, waiting for transfers between devices, local(): lax.all_to_all(jnp.stack([masked] * lax.axis_size('hid')), 'hid', 0, 0)  122 us
    unnamed x3, waiting for transfers between devices  70.4 us
    all_gather x1, waiting for transfers between devices, local(): gathered = lax.all_gather(rounded, 'slot', axis=2, tiled=True)  55.7 us
    unnamed x16, local copies, waits for them, and re-layouts  26.7 us
    dot_general x1, matrix products, local(): lax.dot_general(shard_piece, weight_rows, (((1,), (1,)), ((), ())), prefe...  10 us
    dot_general x1, matrix products, local(): lax.dot_general(hidden, shard_piece, (((0,), (0,)), ((), ())), preferred_...  9.46 us
    convert_element_type x1, other arithmetic, local(): stacked.astype(jnp.bfloat16)  8.01 us
    all_to_all x1, starting transfers between devices, local(): lax.all_to_all(jnp.stack([masked] * lax.axis_size('hid')), 'hid', 0, 0)  7.77 us
  transfers between devices with their start and end apart: 3, of which 3 were waited for; matrix products, arithmetic and copies ran while one was open for 3% of the time, Pallas kernels for 0%

profile of v1, /device:TPU:1, one launch (start us, length us, event | category | flops | bytes accessed | tf_op | source)
XLA Modules:
  0.0 346.4 jit_solution(2620301836180394556)
XLA Ops:
  7.2 0.0 copy-start
  7.2 1.4 dynamic_slice.15
  8.6 0.6 fusion.1
  9.2 1.4 broadcast_multiply_fusion
  10.6 0.2 copy.15
  10.8 4.3 %stack.2 = bf16[16,2048,128]{1,2,0:T(8,128)(2,1)} broadcast(bf16[2048,128]{0,1:T(8,128)(2,1)S(1)} %copy.15), dimensions={1,2} | broadcast | bytes 8912896 | tf_op jit(solution)/shard_map/stack | solution.py:20
  15.2 0.0 copy-start.4
  15.2 7.8 %all-to-all-start = ((bf16[16,2048,128]{1,2,0:T(8,128)(2,1)}), bf16[16,2048,128]{1,2,0:T(8,128)(2,1)}, u32[]{:S(2)}, u32[]{:S(2)}) async-start(bf16[16,2048,128]{1,2,0:T(8,128)(2,1)} %stack.2), calls=%async_computation | async-start | bytes 16777216 | tf_op jit(solution)/shard_map/all_to_all | solution.py:20
  22.9 0.0 reduce-scatter.4.cloned.1.call-start
  23.0 0.0 copy-done.4
  23.0 0.6 dynamic-slice.1
  23.6 0.6 fusion.2
  24.2 121.8 %all-to-all-done = bf16[16,2048,128]{1,2,0:T(8,128)(2,1)} async-done(((bf16[16,2048,128]{1,2,0:T(8,128)(2,1)}), bf16[16,2048,128]{1,2,0:T(8,128)(2,1)}, u32[]{:S(2)}, u32[]{:S(2)}) %all-to-all-start) | async-done | bytes 8388640 | tf_op jit(solution)/shard_map/all_to_all | solution.py:20
  146.1 0.0 copy-done
  146.1 9.5 %convolution_bitcast_fusion = f32[512,2048]{0,1:T(8,128)} fusion(bf16[2048,2048]{0,1:T(8,128)(2,1)} %bitcast.2, bf16[2048,512]{1,0:T(8,128)(2,1)S(1)} %copy-done), kind=kOutput, calls=%fused_computation.1 | convolution fusion | flops 4294967296 | bytes 14680064 | tf_op jit(solution)/shard_map/dot_general | solution.py:25
  155.5 5.4 %copy.16 = f32[512,2048]{1,0:T(8,128)} copy(f32[512,2048]{0,1:T(8,128)} %convolution_bitcast_fusion) | data formatting | bytes 8388608 | tf_op jit(solution)/shard_map/dot_general | solution.py:25
  161.0 8.0 %multiply_convert_fusion = bf16[4,512,2048]{2,1,0:T(8,128)(2,1)} fusion(f32[512,2048]{1,0:T(8,128)} %copy.16, f32[4]{0:T(128)S(1)} %fusion.2), kind=kLoop, calls=%fused_computation | loop fusion | flops 8388608 | bytes 12582928 | tf_op jit(solution)/shard_map/convert_element_type | solution.py:38
  169.0 14.6 %copy.17 = bf16[4,512,2048]{1,0,2:T(4,128)(2,1)} copy(bf16[4,512,2048]{2,1,0:T(8,128)(2,1)} %multiply_convert_fusion) | data formatting | bytes 16777216
  183.6 10.2 %copy.19 = bf16[256,8,4,512]{3,1,2,0:T(8,128)(2,1)} copy(bf16[256,8,4,512]{3,2,1,0:T(4,128)(2,1)} %bitcast.21) | data formatting | bytes 16777216
  193.8 0.0 copy-start.2
  193.8 0.0 copy-start.3
  193.8 0.0 copy-start.5
  193.8 0.0 reduce-scatter.4.cloned.1.call-update
  193.8 0.2 all-gather.2.cloned.1.call-start
  194.1 70.4 %reduce-scatter.4.cloned.1.call-done = bf16[128,2048]{1,0:T(8,128)(2,1)} async-done(((bf16[2048,2048]{1,0:T(8,128)(2,1)}), bf16[128,2048]{1,0:T(8,128)(2,1)}) %reduce-scatter.4.cloned.1.call-update) | async-done | bytes 524304
  264.5 1.4 reshape.31
  265.9 0.4 copy.18
  266.3 0.0 copy-done.2
  266.3 0.0 copy-done.3
  266.3 1.7 fusion.3
  268.0 0.0 all-gather.2.cloned.1.call-update
  268.1 0.0 copy-done.5
  268.1 0.6 constant_dynamic-slice_fusion
  270.6 0.0 copy-start.1
  270.6 10.0 %convolution_convert_fusion = bf16[2048,512]{1,0:T(8,128)(2,1)} fusion(bf16[2048,2048]{0,1:T(8,128)(2,1)} %bitcast.2, bf16[1,512,2048]{2,1,0:T(8,128)(2,1)} %param.10), kind=kOutput, calls=%fused_computation.2 | convolution fusion | flops 4296015872 | bytes 12582912 | tf_op jit(solution)/shard_map/dot_general | solution.py:22
  280.6 55.7 %all-gather.2.cloned.1.call-done = bf16[4,512,2048]{2,1,0:T(8,128)(2,1)} async-done(((bf16[4,512,128]{2,1,0:T(8,128)(2,1)}), bf16[4,512,2048]{2,1,0:T(8,128)(2,1)}) %all-gather.2.cloned.1.call-update) | async-done | bytes 8388624 | tf_op jit(solution)/shard_map/all_gather | solution.py:43
  336.4 3.2 constant_dynamic-slice_fusion.1
  339.5 0.0 copy-done.1
Async XLA Ops:
  7.2 138.9 %copy-start = (bf16[2048,512]{1,0:T(8,128)(2,1)S(1)}, bf16[2048,512]{1,0:T(8,128)(2,1)}, u32[]{:S(2)}) copy-start(bf16[2048,512]{1,0:T(8,128)(2,1)} %param.9) | copy-start | bytes 6291460
  15.2 7.8 %copy-start.4 = (s32[16,1]{0,1:T(1,128)S(1)}, s32[16,1]{0,1:T(1,128)}, u32[]{:S(2)}) copy-start(s32[16,1]{0,1:T(1,128)} %param.11) | copy-start | bytes 196
  15.2 130.9 %all-to-all-start = ((bf16[16,2048,128]{1,2,0:T(8,128)(2,1)}), bf16[16,2048,128]{1,2,0:T(8,128)(2,1)}, u32[]{:S(2)}, u32[]{:S(2)}) async-start(bf16[16,2048,128]{1,2,0:T(8,128)(2,1)} %stack.2), calls=%async_computation | async-start | bytes 16777216 | tf_op jit(solution)/shard_map/all_to_all | solution.py:20
  22.9 241.5 %reduce-scatter.4.cloned.1.call-start = ((), (), s32[]{:S(2)}) async-start(), calls=%async_computation.3 | async-start | bytes 8912896
  193.8 72.5 %copy-start.2 = (f32[4,512,128]{2,1,0:T(8,128)S(1)}, f32[4,512,128]{2,1,0:T(8,128)}, u32[]{:S(2)}) copy-start(f32[4,512,128]{2,1,0:T(8,128)} %param.14) | copy-start | bytes 3145732
  193.8 72.5 %copy-start.3 = (f32[4,512,128]{2,1,0:T(8,128)S(1)}, f32[4,512,128]{2,1,0:T(8,128)}, u32[]{:S(2)}) copy-start(f32[4,512,128]{2,1,0:T(8,128)} %param.15) | copy-start | bytes 3145732
  193.8 74.3 %copy-start.5 = (s32[16,1]{0,1:T(1,128)S(1)}, s32[16,1]{0,1:T(1,128)}, u32[]{:S(2)}) copy-start(s32[16,1]{0,1:T(1,128)} %param.12) | copy-start | bytes 196
  193.8 142.6 %all-gather.2.cloned.1.call-start = ((), (), s32[]{:S(2)}) async-start(), calls=%async_computation.2 | async-start | bytes 8912896 | tf_op jit(solution)/shard_map/all_gather | solution.py:43
  270.6 69.0 %copy-start.1 = (bf16[2048,512]{1,0:T(8,128)(2,1)S(1)}, bf16[2048,512]{1,0:T(8,128)(2,1)}, u32[]{:S(2)}) copy-start(bf16[2048,512]{1,0:T(8,128)(2,1)} %param.9) | copy-start | bytes 6291460
Sparse Core Ops, SparseCore 0:
  193.9 70.4 reduce-scatter.3
  268.2 68.1 all-gather.1
